TPU v7x, 32 devices: a whole 2x2x4 slice. The times are simulated.
32 devices in a mesh: ctx: 2 (over x), kvh: 4 (over z), rep: 4 (over y, core).
Axes of the slice: x: 2, y: 2, z: 4, core: 2. Of those that a mesh axis runs over, the one named last changes fastest.
Arguments:
- query: bfloat16 [256, 16384], P(('rep', 'ctx'), 'kvh'), parts along dimension 0, may hold values from -160 to 160
- slab_keys: bfloat16 [256, 1024], P(('rep', 'ctx'), 'kvh'), parts along dimension 0, may hold values from -6 to 6
- slab_values: bfloat16 [256, 1024], P(('rep', 'ctx'), 'kvh'), parts along dimension 0, may hold values from -6 to 6
- ctx_keys: bfloat16 [16384, 1024], P(('rep', 'ctx'), 'kvh'), parts along dimension 0, may hold values from -7 to 7
- ctx_values: bfloat16 [16384, 1024], P(('rep', 'ctx'), 'kvh'), parts along dimension 0, may hold values from -6 to 6
- prompt_len: int32 [16], P('rep'), parts along dimension 0, may hold values from 2049 to 4096, as said below
- cont_len: int32 [16], P('rep'), parts along dimension 0, may hold values from 1 to 24, 64 in all
- slab_order: int32 [16], P('rep'), parts along dimension 0, may hold values from 0 to 3, as said below
Outputs:
- attention: bfloat16 [256, 16384], P(('rep', 'ctx'), 'kvh'), parts along dimension 0
There are 4 independent parts, one for each index of `rep`. A program takes and returns all parts, laid end to end along the dimension named above; each array names one. Nothing has to cross between parts.
Inputs may be any that keep to these rules, and one draw needn't show every extreme that they name: `prompt_len`: 4 prompt lengths, the largest exactly 4096. `cont_len`: 4 continuation lengths summing to 64, the largest exactly 24. `slab_order`: each span of 0 to 3 once.
All inputs are finite; a program needn't handle non-finite values.
Results may differ from a plain program's by a relative error of at most 0.0044.
Values may be sent and summed in bfloat16 or wider, within the bound.
A program may use at most 128 MiB of HBM per device.

v0:
```python
import math

import jax
import jax.numpy as jnp
from jax import lax
from jax.sharding import PartitionSpec as P

HEADS = 128
KV_HEADS = 8
HEAD_DIM = 128


lowest = -1e30


def rollout_of(positions, ends):
    return jnp.sum((positions[:, None] >= ends[None, :]).astype(jnp.int32), axis=1)


def table_pick(table, index):
    table_ids = jnp.arange(table.shape[0], dtype=jnp.int32)
    return jnp.sum(jnp.where(table_ids[None, :] == index[:, None], table[None, :], 0), axis=1)


def slab_meta(row_ids, slab_order, span_rows, cont_end):
    places = table_pick(slab_order, row_ids // span_rows) * span_rows + row_ids % span_rows
    return (rollout_of(places, cont_end), places)


def context_meta(row_ids):
    return (jnp.full(row_ids.shape, -1, jnp.int32), row_ids)


def empty_state(groups, group, count):
    return (
        jnp.zeros((groups, group, count, HEAD_DIM), jnp.float32),
        jnp.full((groups, group, count), lowest, jnp.float32),
        jnp.zeros((groups, group, count), jnp.float32),
    )


def keep_state(carry):
    return carry


def attend_block(state, query_heads, query_facts, key_block, value_block, key_roll, key_place):
    query_roll, query_place, query_limit = query_facts
    groups = key_block.shape[1] // HEAD_DIM
    key_heads = key_block.reshape(key_block.shape[0], groups, HEAD_DIM)
    value_heads = value_block.reshape(value_block.shape[0], groups, HEAD_DIM)
    in_context = key_roll[None, :] < 0
    same_roll = (key_roll[None, :] == query_roll[:, None]) & (
        key_place[None, :] <= query_place[:, None]
    )
    visible = jnp.where(in_context, key_place[None, :] < query_limit[:, None], same_roll)

    def update(carry):
        numerator, top, total = carry
        scores = jnp.einsum(
            "qghd,kgd->ghqk", query_heads, key_heads, preferred_element_type=jnp.float32
        ) * HEAD_DIM ** (-0.5)
        scores = jnp.where(visible, scores, lowest)
        top_new = jnp.maximum(top, jnp.max(scores, axis=-1))
        weights = jnp.where(visible, jnp.exp(scores - top_new[..., None]), 0.0)
        factor = jnp.exp(top - top_new)
        total = total * factor + jnp.sum(weights, axis=-1)
        numerator = numerator * factor[..., None] + jnp.einsum(
            "ghqk,kgd->ghqd",
            weights.astype(jnp.bfloat16),
            value_heads,
            preferred_element_type=jnp.float32,
        )
        return (numerator, top_new, total)

    return lax.cond(jnp.any(visible), update, keep_state, state)


def fold_keys(state, pieces, meta_fn, query_heads, query_facts):
    key_rows, value_rows = pieces
    count = key_rows.shape[0]
    width = math.gcd(count, 512)
    number = count // width

    def step(block_id, carry):
        offset = block_id * width
        key_block = lax.dynamic_slice_in_dim(key_rows, offset, width, 0)
        value_block = lax.dynamic_slice_in_dim(value_rows, offset, width, 0)
        row_ids = offset + jnp.arange(width, dtype=jnp.int32)
        key_roll, key_place = meta_fn(row_ids)
        return attend_block(
            carry, query_heads, query_facts, key_block, value_block, key_roll, key_place
        )

    return lax.fori_loop(0, number, step, state)


def local(query, slab_keys, slab_values, ctx_keys, ctx_values, prompt_len, cont_len, slab_order):
    query_rows = query.shape[0]
    span_rows = query_rows // 2
    device_index = lax.axis_index("ctx")
    cont_end = jnp.cumsum(cont_len)
    groups = ctx_keys.shape[1] // HEAD_DIM
    group = HEADS // KV_HEADS

    def slab_lookup(row_ids):
        return slab_meta(row_ids, slab_order, span_rows, cont_end)

    own_rows = device_index * query_rows + jnp.arange(query_rows, dtype=jnp.int32)
    roll, place = slab_lookup(own_rows)
    query_facts = (roll, place, table_pick(prompt_len, roll))
    query_heads = query.reshape(query_rows, groups, group, HEAD_DIM)
    state = empty_state(groups, group, query_rows)
    state = fold_keys(
        state,
        (
            lax.all_gather(ctx_keys, "ctx", axis=0, tiled=True),
            lax.all_gather(ctx_values, "ctx", axis=0, tiled=True),
        ),
        context_meta,
        query_heads,
        query_facts,
    )
    state = fold_keys(
        state,
        (
            lax.all_gather(slab_keys, "ctx", axis=0, tiled=True),
            lax.all_gather(slab_values, "ctx", axis=0, tiled=True),
        ),
        slab_lookup,
        query_heads,
        query_facts,
    )
    numerator, top, total = state
    result = numerator / total[..., None]
    return (
        result.transpose(2, 0, 1, 3)
        .reshape(query_rows, groups * group * HEAD_DIM)
        .astype(jnp.bfloat16)
    )


def solution(mesh):
    placed = (
        P(("rep", "ctx"), "kvh"),
        P(("rep", "ctx"), "kvh"),
        P(("rep", "ctx"), "kvh"),
        P(("rep", "ctx"), "kvh"),
        P(("rep", "ctx"), "kvh"),
        P("rep"),
        P("rep"),
        P("rep"),
    )
    return jax.shard_map(
        local, mesh=mesh, in_specs=placed, out_specs=P(("rep", "ctx"), "kvh"), check_vma=False
    )
```

profile of v0, /device:TPU:1, one launch (start us, length us, event | category | flops | bytes accessed | tf_op | source)
XLA Modules:
  0.0 125.8 jit_solution(15081487554473105829)
XLA Ops:
  6.5 2.4 %copy.25 = bf16[2048,256]{0,1:T(8,128)(2,1)} copy(bf16[2048,256]{1,0:T(8,128)(2,1)} %param.17) | data formatting | bytes 2097152 | tf_op args[3]
  9.1 1.4 %copy.26 = bf16[2048,256]{0,1:T(8,128)(2,1)} copy(bf16[2048,256]{1,0:T(8,128)(2,1)S(1)} %copy-done) | data formatting | bytes 2097152 | tf_op args[4]
  11.4 0.7 fusion.27
  12.8 3.8 %all_gather.14 = bf16[64,256]{1,0:T(8,128)(2,1)S(1)} all-gather(bf16[32,256]{1,0:T(8,128)(2,1)S(1)} %copy-done.2), channel_id=1, replica_groups=mesh['ctx'=2,'kvh'=4,'rep'=4] {'ctx'}, dimensions={0}, use_global_device_ids=true | all-gather | bytes 49152 | tf_op jit(solution)/shard_map/all_gather | solution.py:126
  16.6 3.3 %all_gather.15 = bf16[64,256]{1,0:T(8,128)(2,1)S(1)} all-gather(bf16[32,256]{1,0:T(8,128)(2,1)S(1)} %copy-done.3), channel_id=1, replica_groups=mesh['ctx'=2,'kvh'=4,'rep'=4] {'ctx'}, dimensions={0}, use_global_device_ids=true | all-gather | bytes 49152 | tf_op jit(solution)/shard_map/all_gather | solution.py:127
  19.8 24.8 %all-gather.3.cloned.1.call-done = bf16[4096,256]{0,1:T(8,128)(2,1)} async-done(((bf16[2048,256]{0,1:T(8,128)(2,1)}), bf16[4096,256]{0,1:T(8,128)(2,1)}) %all-gather.3.cloned.1.call-update) | async-done | bytes 2097168 | tf_op jit(solution)/shard_map/all_gather | solution.py:116
  44.6 34.5 %all-gather.5.cloned.1.call-done = bf16[4096,256]{0,1:T(8,128)(2,1)} async-done(((bf16[2048,256]{0,1:T(8,128)(2,1)}), bf16[4096,256]{0,1:T(8,128)(2,1)}) %all-gather.5.cloned.1.call-update) | async-done | bytes 2097168 | tf_op jit(solution)/shard_map/all_gather | solution.py:117
  79.2 37.3 %while.4 = (s32[]{:T(128)}, f32[2,16,32,128]{3,2,1,0:T(8,128)S(1)}, f32[2,16,32]{2,1,0:T(8,128)S(1)}, f32[2,16,32]{2,1,0:T(8,128)S(1)}, s32[32]{0:T(128)S(1)}, /...) while((s32[]{:T(128)}, ...), condition=%wide.region_13.14_spmd, body=%wide.region_7.13_spmd.sunk | while | flops 275548672 | bytes 9310617 | solution.py:94
  79.3 0.8 broadcast_compare_fusion.3
  80.8 3.1 %conditional.4 = ((f32[2,16,32,128]{3,2,1,0:T(8,128)S(1)}, f32[2,16,32]{2,1,0:T(8,128)S(1)}, f32[2,16,32]{2,1,0:T(8,128)S(1)})) conditional(s32[]{:T(128)} %convert_element_type.53, (f32[2,16,32,128]{3,2,1,0:T(8,128)S(1)}, f32[2,16,32]{2,1,0:T(8,128)S(1)}, f32[2,16,32]{2,1,0:T(8,128)S(1)}) %tuple.75, (pred[32,512]{1,0:T(8,128)(4,1)S(1)}, s32[]{:T(128)}, ...), branch_computations={%region_9.9_spmd, %region_10.12_spmd} | conditional | flops 275515392 | bytes 9289798 | solution.py:75
  80.8 1.1 constant_dynamic-slice_fusion
  82.4 0.7 fusion.1
  83.1 0.8 convolution_add_fusion
  83.9 0.8 broadcast_compare_fusion.3
  85.4 3.1 %conditional.4 = ((f32[2,16,32,128]{3,2,1,0:T(8,128)S(1)}, f32[2,16,32]{2,1,0:T(8,128)S(1)}, f32[2,16,32]{2,1,0:T(8,128)S(1)})) conditional(s32[]{:T(128)} %convert_element_type.53, (f32[2,16,32,128]{3,2,1,0:T(8,128)S(1)}, f32[2,16,32]{2,1,0:T(8,128)S(1)}, f32[2,16,32]{2,1,0:T(8,128)S(1)}) %tuple.75, (pred[32,512]{1,0:T(8,128)(4,1)S(1)}, s32[]{:T(128)}, ...), branch_computations={%region_9.9_spmd, %region_10.12_spmd} | conditional | flops 275515392 | bytes 9289798 | solution.py:75
  85.5 1.1 constant_dynamic-slice_fusion
  87.0 0.7 fusion.1
  87.7 0.8 convolution_add_fusion
  88.6 0.8 broadcast_compare_fusion.3
  90.1 3.1 %conditional.4 = ((f32[2,16,32,128]{3,2,1,0:T(8,128)S(1)}, f32[2,16,32]{2,1,0:T(8,128)S(1)}, f32[2,16,32]{2,1,0:T(8,128)S(1)})) conditional(s32[]{:T(128)} %convert_element_type.53, (f32[2,16,32,128]{3,2,1,0:T(8,128)S(1)}, f32[2,16,32]{2,1,0:T(8,128)S(1)}, f32[2,16,32]{2,1,0:T(8,128)S(1)}) %tuple.75, (pred[32,512]{1,0:T(8,128)(4,1)S(1)}, s32[]{:T(128)}, ...), branch_computations={%region_9.9_spmd, %region_10.12_spmd} | conditional | flops 275515392 | bytes 9289798 | solution.py:75
  90.1 1.1 constant_dynamic-slice_fusion
  91.7 0.7 fusion.1
  92.4 0.8 convolution_add_fusion
  93.3 0.8 broadcast_compare_fusion.3
  94.8 3.1 %conditional.4 = ((f32[2,16,32,128]{3,2,1,0:T(8,128)S(1)}, f32[2,16,32]{2,1,0:T(8,128)S(1)}, f32[2,16,32]{2,1,0:T(8,128)S(1)})) conditional(s32[]{:T(128)} %convert_element_type.53, (f32[2,16,32,128]{3,2,1,0:T(8,128)S(1)}, f32[2,16,32]{2,1,0:T(8,128)S(1)}, f32[2,16,32]{2,1,0:T(8,128)S(1)}) %tuple.75, (pred[32,512]{1,0:T(8,128)(4,1)S(1)}, s32[]{:T(128)}, ...), branch_computations={%region_9.9_spmd, %region_10.12_spmd} | conditional | flops 275515392 | bytes 9289798 | solution.py:75
  94.8 1.1 constant_dynamic-slice_fusion
  96.4 0.7 fusion.1
  97.1 0.8 convolution_add_fusion
  97.9 0.8 broadcast_compare_fusion.3
  99.4 3.1 %conditional.4 = ((f32[2,16,32,128]{3,2,1,0:T(8,128)S(1)}, f32[2,16,32]{2,1,0:T(8,128)S(1)}, f32[2,16,32]{2,1,0:T(8,128)S(1)})) conditional(s32[]{:T(128)} %convert_element_type.53, (f32[2,16,32,128]{3,2,1,0:T(8,128)S(1)}, f32[2,16,32]{2,1,0:T(8,128)S(1)}, f32[2,16,32]{2,1,0:T(8,128)S(1)}) %tuple.75, (pred[32,512]{1,0:T(8,128)(4,1)S(1)}, s32[]{:T(128)}, ...), branch_computations={%region_9.9_spmd, %region_10.12_spmd} | conditional | flops 275515392 | bytes 9289798 | solution.py:75
  99.4 1.1 constant_dynamic-slice_fusion
  101.0 0.7 fusion.1
  101.7 0.8 convolution_add_fusion
  102.6 0.8 broadcast_compare_fusion.3
  104.1 3.1 %conditional.4 = ((f32[2,16,32,128]{3,2,1,0:T(8,128)S(1)}, f32[2,16,32]{2,1,0:T(8,128)S(1)}, f32[2,16,32]{2,1,0:T(8,128)S(1)})) conditional(s32[]{:T(128)} %convert_element_type.53, (f32[2,16,32,128]{3,2,1,0:T(8,128)S(1)}, f32[2,16,32]{2,1,0:T(8,128)S(1)}, f32[2,16,32]{2,1,0:T(8,128)S(1)}) %tuple.75, (pred[32,512]{1,0:T(8,128)(4,1)S(1)}, s32[]{:T(128)}, ...), branch_computations={%region_9.9_spmd, %region_10.12_spmd} | conditional | flops 275515392 | bytes 9289798 | solution.py:75
  104.1 1.1 constant_dynamic-slice_fusion
  106.4 0.8 convolution_add_fusion
  107.2 0.8 broadcast_compare_fusion.3
  108.7 3.1 %conditional.4 = ((f32[2,16,32,128]{3,2,1,0:T(8,128)S(1)}, f32[2,16,32]{2,1,0:T(8,128)S(1)}, f32[2,16,32]{2,1,0:T(8,128)S(1)})) conditional(s32[]{:T(128)} %convert_element_type.53, (f32[2,16,32,128]{3,2,1,0:T(8,128)S(1)}, f32[2,16,32]{2,1,0:T(8,128)S(1)}, f32[2,16,32]{2,1,0:T(8,128)S(1)}) %tuple.75, (pred[32,512]{1,0:T(8,128)(4,1)S(1)}, s32[]{:T(128)}, ...), branch_computations={%region_9.9_spmd, %region_10.12_spmd} | conditional | flops 275515392 | bytes 9289798 | solution.py:75
  108.8 1.1 constant_dynamic-slice_fusion
  111.0 0.8 convolution_add_fusion
  111.9 0.8 broadcast_compare_fusion.3
  113.4 3.1 %conditional.4 = ((f32[2,16,32,128]{3,2,1,0:T(8,128)S(1)}, f32[2,16,32]{2,1,0:T(8,128)S(1)}, f32[2,16,32]{2,1,0:T(8,128)S(1)})) conditional(s32[]{:T(128)} %convert_element_type.53, (f32[2,16,32,128]{3,2,1,0:T(8,128)S(1)}, f32[2,16,32]{2,1,0:T(8,128)S(1)}, f32[2,16,32]{2,1,0:T(8,128)S(1)}) %tuple.75, (pred[32,512]{1,0:T(8,128)(4,1)S(1)}, s32[]{:T(128)}, ...), branch_computations={%region_9.9_spmd, %region_10.12_spmd} | conditional | flops 275515392 | bytes 9289798 | solution.py:75
  113.4 1.1 constant_dynamic-slice_fusion
  115.0 0.7 fusion.1
  115.7 0.8 convolution_add_fusion
  116.5 1.3 %conditional.2 = ((f32[2,16,32,128]{3,2,1,0:T(8,128)S(1)}, f32[2,16,32]{2,1,0:T(8,128)S(1)})) conditional(s32[]{:T(128)} %convert_element_type.39, (f32[2,16,32,128]{3,2,1,0:T(8,128)S(1)}, f32[2,16,32]{2,1,0:T(8,128)S(1)}) %tuple.50, (pred[32,64]{1,0:T(8,128)(4,1)S(1)}, bf16[64,256]{1,0:T(8,128)(2,1)S(1)}, bf16[32,2,16,128]{3,2,1,0:T(8,128)(2,1)S(1)}, ...), branch_computations={%region_14.15_spmd, %region_15.18_spmd} | conditional | flops 34408448 | bytes 2357272 | solution.py:75
  118.1 0.8 copy.55
  (85 shorter events, 8.1 us)
Async XLA Ops:
  6.5 2.5 %copy-start = (bf16[2048,256]{1,0:T(8,128)(2,1)S(1)}, bf16[2048,256]{1,0:T(8,128)(2,1)}, u32[]{:S(2)}) copy-start(bf16[2048,256]{1,0:T(8,128)(2,1)} %param.18) | copy-start | bytes 3145732
  6.5 38.1 %all-gather.3.cloned.1.call-start = ((), (), s32[]{:S(2)}) async-start(), calls=%async_computation | async-start | bytes 3145728 | tf_op jit(solution)/shard_map/all_gather | solution.py:116
  8.9 1.6 %copy-start.1 = (bf16[32,4096]{1,0:T(8,128)(2,1)S(1)}, bf16[32,4096]{1,0:T(8,128)(2,1)}, u32[]{:S(2)}) copy-start(bf16[32,4096]{1,0:T(8,128)(2,1)} %param.14) | copy-start | bytes 786436
  8.9 1.8 %copy-start.4 = (s32[4]{0:T(128)S(1)}, s32[4]{0:T(128)}, u32[]{:S(2)}) copy-start(s32[4]{0:T(128)} %param.20) | copy-start | bytes 52
  9.0 2.0 %copy-start.5 = (s32[4]{0:T(128)S(1)}, s32[4]{0:T(128)}, u32[]{:S(2)}) copy-start(s32[4]{0:T(128)} %param.21) | copy-start | bytes 52
  9.0 2.3 %copy-start.6 = (s32[4]{0:T(128)S(1)}, s32[4]{0:T(128)}, u32[]{:S(2)}) copy-start(s32[4]{0:T(128)} %param.19) | copy-start | bytes 52
  9.0 3.8 %copy-start.2 = (bf16[32,256]{1,0:T(8,128)(2,1)S(1)}, bf16[32,256]{1,0:T(8,128)(2,1)}, u32[]{:S(2)}) copy-start(bf16[32,256]{1,0:T(8,128)(2,1)} %param.15) | copy-start | bytes 49156
  9.0 7.6 %copy-start.3 = (bf16[32,256]{1,0:T(8,128)(2,1)S(1)}, bf16[32,256]{1,0:T(8,128)(2,1)}, u32[]{:S(2)}) copy-start(bf16[32,256]{1,0:T(8,128)(2,1)} %param.16) | copy-start | bytes 49156
  9.0 70.2 %all-gather.5.cloned.1.call-start = ((), (), s32[]{:S(2)}) async-start(), calls=%async_computation.1 | async-start | bytes 3145728 | tf_op jit(solution)/shard_map/all_gather | solution.py:117
Sparse Core Ops, SparseCore 0:
  9.1 35.5 all-gather.2
  46.2 32.9 all-gather.4
where the time goes:
time: 126 us
  waiting for transfers between devices  59.3 us (47%)
  between operations  14.2 us (11%)
  other arithmetic  13.9 us (11%)
  local copies, waits for them, and re-layouts  13.6 us (11%)
  matrix products  11.3 us (9%)
  blocking collectives  7.07 us (6%)
  loops' own time  6.33 us (5%)
    all_gather x1, waiting for transfers between devices, local(): lax.all_gather(ctx_values, 'ctx', axis=0, tiled=True)  34.5 us
    all_gather x1, waiting for transfers between devices, local(): lax.all_gather(ctx_keys, 'ctx', axis=0, tiled=True)  24.8 us
    dynamic_slice x8, local copies, waits for them, and re-layouts, step(): value_block = lax.dynamic_slice_in_dim(value_rows, offset, width, 0)  8.57 us
    dot_general x9, matrix products, update(): jnp.einsum('ghqk,kgd->ghqd', weights.astype(jnp.bfloat16), value_heads, p...  6.88 us
    lt x8, other arithmetic, attend_block(): key_place[None, :] < query_limit[:, None]  6.4 us
    another operation x1, loops' own time, fold_keys(): return lax.fori_loop(0, number, step, state)  5.84 us
    reduce_sum x9, other arithmetic, update(): total = total * factor + jnp.sum(weights, axis=-1)  5.67 us
    unnamed x18, local copies, waits for them, and re-layouts  4.71 us
  transfers between devices with their start and end apart: 2, of which 2 were waited for; matrix products, arithmetic and copies ran while one was open for 2% of the time, Pallas kernels for 0%

commit v1 on v0

v1 whole, which is shorter than its diff:
```python
import jax
import jax.numpy as jnp
from jax import lax
from jax.experimental import pallas as pl
from jax.experimental.pallas import tpu as pltpu
from jax.sharding import PartitionSpec as P

HEADS = 128
KV_HEADS = 8
HEAD_DIM = 128
GROUP = HEADS // KV_HEADS
LOG2E = 1.4426950408889634
SCALE2 = HEAD_DIM ** -0.5 * LOG2E
LOWEST = -1e30
MESH = pl.DeviceIdType.MESH

CHUNK_HEADS = 8
LEAD = 2


def make_kernel(n, rows, cols, keys, spans):
    groups = cols // (GROUP * HEAD_DIM)
    width = CHUNK_HEADS * HEAD_DIM
    chunks = cols // width
    per_group = chunks // groups
    span = rows * n // spans
    local_spans = rows // span
    total_items = n * chunks
    own = n - 1
    lead = LEAD

    def kernel(prompt_ref, cont_ref, order_ref, q_hbm, sk_hbm, sv_hbm, ck_hbm, cv_hbm, out_ref,
               qbuf, kbuf, vbuf, skbuf, svbuf, osend, orecv, oown, lse, lrecv,
               local_sem, q_send, q_recv, o_send, o_recv, l_send, l_recv):
        me = lax.axis_index("ctx")

        local_copies = []
        for g in range(groups):
            lanes = slice(g * HEAD_DIM, (g + 1) * HEAD_DIM)
            for i, (src, dst) in enumerate((
                (ck_hbm.at[:, lanes], kbuf.at[g]),
                (cv_hbm.at[:, lanes], vbuf.at[g]),
                (sk_hbm.at[:, lanes], skbuf.at[g, 0:rows]),
                (sv_hbm.at[:, lanes], svbuf.at[g, 0:rows]),
            )):
                local_copies.append(pltpu.make_async_copy(src, dst, local_sem.at[g * 4 + i]))
        local_copies.append(pltpu.make_async_copy(q_hbm, qbuf.at[own], local_sem.at[groups * 4]))
        for copy in local_copies:
            copy.start()

        barrier = pltpu.get_barrier_semaphore()
        for d in range(1, n):
            pl.semaphore_signal(barrier, inc=1, device_id={"ctx": lax.rem(me + d, n)}, device_id_type=MESH)

        pad = skbuf.shape[1] - rows
        for g in range(groups):
            skbuf[g, rows:, :] = jnp.zeros((pad, HEAD_DIM), jnp.bfloat16)
            svbuf[g, rows:, :] = jnp.zeros((pad, HEAD_DIM), jnp.bfloat16)

        pl.semaphore_wait(barrier, n - 1)

        def q_copy(slot, c):
            at = pl.ds(pl.multiple_of(c * width, width), width)
            return pltpu.make_async_remote_copy(
                src_ref=q_hbm.at[:, at], dst_ref=qbuf.at[slot, :, at],
                send_sem=q_send.at[slot, c], recv_sem=q_recv.at[slot, c],
                device_id={"ctx": lax.rem(me + slot + 1, n)}, device_id_type=MESH)

        def o_copy(slot, c):
            at = pl.ds(pl.multiple_of(c * width, width), width)
            return pltpu.make_async_remote_copy(
                src_ref=osend.at[slot, :, at], dst_ref=orecv.at[slot, :, at],
                send_sem=o_send.at[slot, c], recv_sem=o_recv.at[slot, c],
                device_id={"ctx": lax.rem(me + 2 * n - slot - 1, n)}, device_id_type=MESH)

        def l_copy(slot):
            return pltpu.make_async_remote_copy(
                src_ref=lse.at[slot], dst_ref=lrecv.at[slot],
                send_sem=l_send.at[slot], recv_sem=l_recv.at[slot],
                device_id={"ctx": lax.rem(me + 2 * n - slot - 1, n)}, device_id_type=MESH)

        for slot in range(n - 1):
            for c in range(chunks):
                q_copy(slot, c).start()
        for copy in local_copies:
            copy.wait()

        ends, prompts, at_end = [], [], 0
        for r in range(prompt_ref.shape[0]):
            at_end = at_end + cont_ref[r]
            ends.append(at_end)
            prompts.append(prompt_ref[r])

        def facts(shape, dim, device):
            ids = lax.broadcasted_iota(jnp.int32, shape, dim)
            place = ids
            for k in range(local_spans):
                start = order_ref[device * local_spans + k] * span - k * span
                inside = (ids >= k * span) & (ids < (k + 1) * span)
                place = jnp.where(inside, ids + start, place)
            roll = jnp.zeros(shape, jnp.int32)
            for end in ends:
                roll = roll + (place >= end).astype(jnp.int32)
            return place, roll

        key_place, key_roll = facts((rows, skbuf.shape[1]), 1, me)
        key_is = lax.broadcasted_iota(jnp.int32, (rows, skbuf.shape[1]), 1) < rows
        lane = lax.broadcasted_iota(jnp.int32, (rows, 128), 1)

        def step(t, carry):
            item = lax.rem(t + total_items - lead, total_items)
            slot = item // chunks
            c = lax.rem(item, chunks)
            g = c // per_group
            source = lax.rem(me + 2 * n - slot - 1, n)

            @pl.when(slot < own)
            def _():
                q_copy(slot, c).wait_recv()

            row_place, row_roll = facts((rows, 128), 0, source)
            limit = jnp.zeros((rows, 128), jnp.int32)
            for r, prompt in enumerate(prompts):
                limit = jnp.where(row_roll == r, prompt, limit)
            limit = limit[:, :1] - me * keys
            slab_bias = jnp.where(
                key_is & (key_roll == row_roll) & (key_place <= row_place), 0.0, LOWEST)

            at = pl.ds(pl.multiple_of(c * width, width), width)
            q = qbuf[slot, :, at]
            q = jnp.concatenate(
                [q[:, h * HEAD_DIM:(h + 1) * HEAD_DIM] for h in range(CHUNK_HEADS)], axis=0)
            dims = (((1,), (1,)), ((), ()))
            s_ctx = lax.dot_general(q, kbuf[g], dims, preferred_element_type=jnp.float32)
            s_slab = lax.dot_general(q, skbuf[g], dims, preferred_element_type=jnp.float32)
            limits = jnp.concatenate([limit] * CHUNK_HEADS, axis=0)
            columns = lax.broadcasted_iota(jnp.int32, s_ctx.shape, 1)
            s_ctx = jnp.where(columns < limits, s_ctx, LOWEST)
            s_slab = s_slab + jnp.concatenate([slab_bias] * CHUNK_HEADS, axis=0)
            top = jnp.maximum(
                jnp.max(s_ctx, axis=1, keepdims=True), jnp.max(s_slab, axis=1, keepdims=True))
            p_ctx = jnp.exp2((s_ctx - top) * SCALE2)
            p_slab = jnp.exp2((s_slab - top) * SCALE2)
            total = jnp.sum(p_ctx, axis=1, keepdims=True) + jnp.sum(p_slab, axis=1, keepdims=True)
            o = jnp.dot(p_ctx.astype(jnp.bfloat16), vbuf[g], preferred_element_type=jnp.float32)
            o = o + jnp.dot(p_slab.astype(jnp.bfloat16), svbuf[g], preferred_element_type=jnp.float32)
            o = o * (1.0 / total)
            level = top * SCALE2 + jnp.log2(total)
            levels = lse[slot]
            for h in range(CHUNK_HEADS):
                levels = jnp.where(
                    lane == c * CHUNK_HEADS + h, level[h * rows:(h + 1) * rows], levels)
            lse[slot] = levels
            o = jnp.concatenate(
                [o[h * rows:(h + 1) * rows] for h in range(CHUNK_HEADS)], axis=1)

            @pl.when(slot == own)
            def _():
                oown[:, at] = o

            @pl.when(slot < own)
            def _():
                osend[slot, :, at] = o.astype(jnp.bfloat16)
                o_copy(slot, c).start()

                @pl.when(c == chunks - 1)
                def _():
                    l_copy(slot).start()

            return carry

        for slot in range(n):
            lse[slot] = jnp.zeros((rows, 128), jnp.float32)
        lax.fori_loop(0, total_items, step, 0)

        for slot in range(n - 1):
            for c in range(chunks):
                o_copy(slot, c).wait_recv()
            l_copy(slot).wait_recv()
        levels = [lrecv[slot] for slot in range(n - 1)] + [lse[own]]
        top = levels[0]
        for level in levels[1:]:
            top = jnp.maximum(top, level)
        shares = [jnp.exp2(level - top) for level in levels]
        whole = shares[0]
        for share in shares[1:]:
            whole = whole + share
        shares = [share / whole for share in shares]
        for h in range(cols // HEAD_DIM):
            at = slice(h * HEAD_DIM, (h + 1) * HEAD_DIM)
            mixed = oown[:, at] * shares[own][:, h:h + 1]
            for slot in range(n - 1):
                mixed = mixed + orecv[slot, :, at].astype(jnp.float32) * shares[slot][:, h:h + 1]
            out_ref[:, at] = mixed.astype(jnp.bfloat16)
        for slot in range(n - 1):
            for c in range(chunks):
                q_copy(slot, c).wait_send()
                o_copy(slot, c).wait_send()
            l_copy(slot).wait_send()

    return kernel, chunks, groups


def solution(mesh):
    n = mesh.shape["ctx"]

    def local(query, slab_keys, slab_values, ctx_keys, ctx_values, prompt_len, cont_len, slab_order):
        rows, cols = query.shape
        keys = ctx_keys.shape[0]
        kernel, chunks, groups = make_kernel(n, rows, cols, keys, slab_order.shape[0])
        slab_pad = -(-rows // 128) * 128
        smem = pl.BlockSpec(memory_space=pltpu.SMEM)
        anywhere = pl.BlockSpec(memory_space=pl.ANY)
        bf16, f32 = jnp.bfloat16, jnp.float32
        dma = pltpu.SemaphoreType.DMA
        return pl.pallas_call(
            kernel,
            out_shape=jax.ShapeDtypeStruct((rows, cols), bf16),
            in_specs=[smem] * 3 + [anywhere] * 5,
            out_specs=pl.BlockSpec(memory_space=pltpu.VMEM),
            scratch_shapes=[
                pltpu.VMEM((n, rows, cols), bf16),
                pltpu.VMEM((groups, keys, HEAD_DIM), bf16),
                pltpu.VMEM((groups, keys, HEAD_DIM), bf16),
                pltpu.VMEM((groups, slab_pad, HEAD_DIM), bf16),
                pltpu.VMEM((groups, slab_pad, HEAD_DIM), bf16),
                pltpu.VMEM((n - 1, rows, cols), bf16),
                pltpu.VMEM((n - 1, rows, cols), bf16),
                pltpu.VMEM((rows, cols), f32),
                pltpu.VMEM((n, rows, 128), f32),
                pltpu.VMEM((n - 1, rows, 128), f32),
                dma((4 * groups + 1,)),
                dma((n - 1, chunks)),
                dma((n - 1, chunks)),
                dma((n - 1, chunks)),
                dma((n - 1, chunks)),
                dma((n - 1,)),
                dma((n - 1,)),
            ],
            compiler_params=pltpu.CompilerParams(
                collective_id=0, has_side_effects=True, vmem_limit_bytes=56 * 1024 * 1024),
        )(prompt_len, cont_len, slab_order, query, slab_keys, slab_values, ctx_keys, ctx_values)

    placed = (P(("rep", "ctx"), "kvh"),) * 5 + (P("rep"),) * 3
    return jax.shard_map(
        local, mesh=mesh, in_specs=placed, out_specs=P(("rep", "ctx"), "kvh"), check_vma=False)
```

time: 126 us -> 19.9 us (0.16)
  the two profiles are of different devices: /device:TPU:1 before, /device:TPU:0 now
where the time goes in v1:
time: 19.9 us; the launch traced here: 19.8 us
  Pallas kernels  18.1 us (91%)
  local copies, waits for them, and re-layouts  1.67 us (8%)
    pallas_call x1, Pallas kernels, local(): pl.pallas_call(kernel, out_shape=jax.ShapeDtypeStruct((rows, cols), bf16)...  18.1 us
    unnamed x1, local copies, waits for them, and re-layouts  1.67 us

profile of v1, /device:TPU:0, one launch (start us, length us, event | category | flops | bytes accessed | tf_op | source)
XLA Modules:
  0.0 19.8 jit_solution(6848867674018642139)
XLA Ops:
  0.0 18.1 %shard_map.82 = bf16[32,4096]{1,0:T(8,128)(2,1)} custom-call(s32[4]{0:T(128)} %prompt_ref.1, s32[4]{0:T(128)} %cont_ref.1, s32[4]{0:T(128)} %order_ref.1, bf16[32,4096]{1,0:T(8,128)(2,1)} %q_hbm.1, bf16[32,256]{1,0:T(8,128)(2,1)} %sk_hbm.1, bf16[32,256]{1,0:T(8,128)(2,1)} %sv_hbm.1, bf16[2048,256]{1,0:T(8,128)(2,1)} %ck_hbm.1, bf16[2048,256]{1,0:T(8,128)(2,1)} %cv_hbm.1), custom_call_target="tpu_custom_call" | custom-call | tf_op jit(solution)/shard_map/pallas_call | solution.py:216
  18.1 1.7 %copy.10 = bf16[32,4096]{1,0:T(8,128)(2,1)} copy(bf16[32,4096]{1,0:T(8,128)(2,1)} %shard_map.82) | data formatting | bytes 524288

commit v2 on v1

--- a/solution.py
+++ b/solution.py
@@ -29,10 +29,14 @@
     own = n - 1
     lead = LEAD
 
-    def kernel(prompt_ref, cont_ref, order_ref, q_hbm, sk_hbm, sv_hbm, ck_hbm, cv_hbm, out_ref,
-               qbuf, kbuf, vbuf, skbuf, svbuf, osend, orecv, oown, lse, lrecv,
+    def kernel(prompt_hbm, cont_hbm, order_hbm, q_hbm, sk_hbm, sv_hbm, ck_hbm, cv_hbm, out_ref,
+               prompt_ref, cont_ref, order_ref, qbuf, kbuf, vbuf, skbuf, svbuf, osend, orecv, oown, lse, lrecv,
                local_sem, q_send, q_recv, o_send, o_recv, l_send, l_recv):
         me = lax.axis_index("ctx")
+
+        barrier = pltpu.get_barrier_semaphore()
+        for d in range(1, n):
+            pl.semaphore_signal(barrier, inc=1, device_id={"ctx": lax.rem(me + d, n)}, device_id_type=MESH)
 
         local_copies = []
         for g in range(groups):
@@ -45,12 +49,11 @@
             )):
                 local_copies.append(pltpu.make_async_copy(src, dst, local_sem.at[g * 4 + i]))
         local_copies.append(pltpu.make_async_copy(q_hbm, qbuf.at[own], local_sem.at[groups * 4]))
+        for i, (src, dst) in enumerate((
+            (prompt_hbm, prompt_ref), (cont_hbm, cont_ref), (order_hbm, order_ref))):
+            local_copies.append(pltpu.make_async_copy(src, dst, local_sem.at[groups * 4 + 1 + i]))
         for copy in local_copies:
             copy.start()
-
-        barrier = pltpu.get_barrier_semaphore()
-        for d in range(1, n):
-            pl.semaphore_signal(barrier, inc=1, device_id={"ctx": lax.rem(me + d, n)}, device_id_type=MESH)
 
         pad = skbuf.shape[1] - rows
         for g in range(groups):
@@ -209,16 +212,18 @@
         keys = ctx_keys.shape[0]
         kernel, chunks, groups = make_kernel(n, rows, cols, keys, slab_order.shape[0])
         slab_pad = -(-rows // 128) * 128
-        smem = pl.BlockSpec(memory_space=pltpu.SMEM)
         anywhere = pl.BlockSpec(memory_space=pl.ANY)
         bf16, f32 = jnp.bfloat16, jnp.float32
         dma = pltpu.SemaphoreType.DMA
         return pl.pallas_call(
             kernel,
-            out_shape=jax.ShapeDtypeStruct((rows, cols), bf16),
-            in_specs=[smem] * 3 + [anywhere] * 5,
+            out_shape=pltpu.VMEM((rows, cols), bf16),
+            in_specs=[anywhere] * 8,
             out_specs=pl.BlockSpec(memory_space=pltpu.VMEM),
             scratch_shapes=[
+                pltpu.SMEM(prompt_len.shape, jnp.int32),
+                pltpu.SMEM(cont_len.shape, jnp.int32),
+                pltpu.SMEM(slab_order.shape, jnp.int32),
                 pltpu.VMEM((n, rows, cols), bf16),
                 pltpu.VMEM((groups, keys, HEAD_DIM), bf16),
                 pltpu.VMEM((groups, keys, HEAD_DIM), bf16),
@@ -229,7 +234,7 @@
                 pltpu.VMEM((rows, cols), f32),
                 pltpu.VMEM((n, rows, 128), f32),
                 pltpu.VMEM((n - 1, rows, 128), f32),
-                dma((4 * groups + 1,)),
+                dma((4 * groups + 4,)),
                 dma((n - 1, chunks)),
                 dma((n - 1, chunks)),
                 dma((n - 1, chunks)),

time: 19.9 us -> 17.6 us (0.88)
  Pallas kernels: 18.1 us -> 16.7 us
  local copies, waits for them, and re-layouts: 1.67 us -> 0.71 us
    pallas_call x1, Pallas kernels: 18.1 us -> 16.7 us  [local(): pl.pallas_call(kernel, out_shape=pltpu.VMEM((rows, cols), bf16), in_specs...]
    unnamed x1, local copies, waits for them, and re-layouts: 1.67 us -> 0.71 us
where the time goes in v2:
time: 17.6 us; the launch traced here: 17.4 us
  Pallas kernels  16.7 us (95%)
  local copies, waits for them, and re-layouts  0.71 us (4%)
    pallas_call x1, Pallas kernels, local(): pl.pallas_call(kernel, out_shape=pltpu.VMEM((rows, cols), bf16), in_specs...  16.7 us
    unnamed x1, local copies, waits for them, and re-layouts  0.71 us

profile of v2, /device:TPU:0, one launch (start us, length us, event | category | flops | bytes accessed | tf_op | source)
XLA Modules:
  0.0 17.4 jit_solution(4572788246396330182)
XLA Ops:
  0.0 16.7 %shard_map.82 = bf16[32,4096]{1,0:T(8,128)(2,1)S(1)} custom-call(s32[4]{0:T(128)} %prompt_hbm.1, s32[4]{0:T(128)} %cont_hbm.1, s32[4]{0:T(128)} %order_hbm.1, bf16[32,4096]{1,0:T(8,128)(2,1)} %q_hbm.1, bf16[32,256]{1,0:T(8,128)(2,1)} %sk_hbm.1, bf16[32,256]{1,0:T(8,128)(2,1)} %sv_hbm.1, bf16[2048,256]{1,0:T(8,128)(2,1)} %ck_hbm.1, bf16[2048,256]{1,0:T(8,128)(2,1)} %cv_hbm.1), custom_call_target="tpu_custom_call" | custom-call | tf_op jit(solution)/shard_map/pallas_call | solution.py:218
  16.7 0.7 %copy.10 = bf16[32,4096]{1,0:T(8,128)(2,1)} copy(bf16[32,4096]{1,0:T(8,128)(2,1)S(1)} %shard_map.82) | data formatting | bytes 524288

commit v3 on v2

--- a/solution.py
+++ b/solution.py
@@ -27,6 +27,9 @@
     local_spans = rows // span
     total_items = n * chunks
     own = n - 1
+    heads = cols // HEAD_DIM
+    side = 128 // heads
+    blocks = rows // 8
     lead = LEAD
 
     def kernel(prompt_hbm, cont_hbm, order_hbm, q_hbm, sk_hbm, sv_hbm, ck_hbm, cv_hbm, out_ref,
@@ -108,7 +111,7 @@
 
         key_place, key_roll = facts((rows, skbuf.shape[1]), 1, me)
         key_is = lax.broadcasted_iota(jnp.int32, (rows, skbuf.shape[1]), 1) < rows
-        lane = lax.broadcasted_iota(jnp.int32, (rows, 128), 1)
+        lane = lax.broadcasted_iota(jnp.int32, (8, 128), 1)
 
         def step(t, carry):
             item = lax.rem(t + total_items - lead, total_items)
@@ -149,11 +152,14 @@
             o = o + jnp.dot(p_slab.astype(jnp.bfloat16), svbuf[g], preferred_element_type=jnp.float32)
             o = o * (1.0 / total)
             level = top * SCALE2 + jnp.log2(total)
-            levels = lse[slot]
-            for h in range(CHUNK_HEADS):
-                levels = jnp.where(
-                    lane == c * CHUNK_HEADS + h, level[h * rows:(h + 1) * rows], levels)
-            lse[slot] = levels
+            for band in range(lse.shape[1] // 8):
+                levels = lse[slot, band * 8:band * 8 + 8]
+                for h in range(CHUNK_HEADS):
+                    for k in range(side):
+                        first = h * rows + (band * side + k) * 8
+                        levels = jnp.where(
+                            lane == k * heads + c * CHUNK_HEADS + h, level[first:first + 8], levels)
+                lse[slot, band * 8:band * 8 + 8] = levels
             o = jnp.concatenate(
                 [o[h * rows:(h + 1) * rows] for h in range(CHUNK_HEADS)], axis=1)
 
@@ -164,21 +170,20 @@
             @pl.when(slot < own)
             def _():
                 osend[slot, :, at] = o.astype(jnp.bfloat16)
-                o_copy(slot, c).start()
 
                 @pl.when(c == chunks - 1)
                 def _():
                     l_copy(slot).start()
 
+                o_copy(slot, c).start()
+
             return carry
 
         for slot in range(n):
-            lse[slot] = jnp.zeros((rows, 128), jnp.float32)
+            lse[slot] = jnp.zeros(lse.shape[1:], jnp.float32)
         lax.fori_loop(0, total_items, step, 0)
 
         for slot in range(n - 1):
-            for c in range(chunks):
-                o_copy(slot, c).wait_recv()
             l_copy(slot).wait_recv()
         levels = [lrecv[slot] for slot in range(n - 1)] + [lse[own]]
         top = levels[0]
@@ -189,11 +194,20 @@
         for share in shares[1:]:
             whole = whole + share
         shares = [share / whole for share in shares]
-        for h in range(cols // HEAD_DIM):
+
+        def share_of(slot, h):
+            return jnp.concatenate([
+                shares[slot][k // side * 8:k // side * 8 + 8, k % side * heads + h:k % side * heads + h + 1]
+                for k in range(blocks)], axis=0)
+
+        for h in range(heads):
+            if h % CHUNK_HEADS == 0:
+                for slot in range(n - 1):
+                    o_copy(slot, h // CHUNK_HEADS).wait_recv()
             at = slice(h * HEAD_DIM, (h + 1) * HEAD_DIM)
-            mixed = oown[:, at] * shares[own][:, h:h + 1]
+            mixed = oown[:, at] * share_of(own, h)
             for slot in range(n - 1):
-                mixed = mixed + orecv[slot, :, at].astype(jnp.float32) * shares[slot][:, h:h + 1]
+                mixed = mixed + orecv[slot, :, at].astype(jnp.float32) * share_of(slot, h)
             out_ref[:, at] = mixed.astype(jnp.bfloat16)
         for slot in range(n - 1):
             for c in range(chunks):
@@ -211,6 +225,7 @@
         rows, cols = query.shape
         keys = ctx_keys.shape[0]
         kernel, chunks, groups = make_kernel(n, rows, cols, keys, slab_order.shape[0])
+        level_rows = rows * (cols // HEAD_DIM) // 128
         slab_pad = -(-rows // 128) * 128
         anywhere = pl.BlockSpec(memory_space=pl.ANY)
         bf16, f32 = jnp.bfloat16, jnp.float32
@@ -232,8 +247,8 @@
                 pltpu.VMEM((n - 1, rows, cols), bf16),
                 pltpu.VMEM((n - 1, rows, cols), bf16),
                 pltpu.VMEM((rows, cols), f32),
-                pltpu.VMEM((n, rows, 128), f32),
-                pltpu.VMEM((n - 1, rows, 128), f32),
+                pltpu.VMEM((n, level_rows, 128), f32),
+                pltpu.VMEM((n - 1, level_rows, 128), f32),
                 dma((4 * groups + 4,)),
                 dma((n - 1, chunks)),
                 dma((n - 1, chunks)),

time: 17.6 us -> 17.2 us (0.977)
  Pallas kernels: 16.7 us -> 16.3 us
    pallas_call x1, Pallas kernels: 16.7 us -> 16.3 us  [local(): pl.pallas_call(kernel, out_shape=pltpu.VMEM((rows, cols), bf16), in_specs...]
where the time goes in v3:
time: 17.2 us; the launch traced here: 17 us
  Pallas kernels  16.3 us (95%)
  local copies, waits for them, and re-layouts  0.71 us (4%)
    pallas_call x1, Pallas kernels, local(): pl.pallas_call(kernel, out_shape=pltpu.VMEM((rows, cols), bf16), in_specs...  16.3 us
    unnamed x1, local copies, waits for them, and re-layouts  0.71 us

profile of v3, /device:TPU:0, one launch (start us, length us, event | category | flops | bytes accessed | tf_op | source)
XLA Modules:
  0.0 17.0 jit_solution(18410151280786986193)
XLA Ops:
  0.0 16.3 %shard_map.82 = bf16[32,4096]{1,0:T(8,128)(2,1)S(1)} custom-call(s32[4]{0:T(128)} %prompt_hbm.1, s32[4]{0:T(128)} %cont_hbm.1, s32[4]{0:T(128)} %order_hbm.1, bf16[32,4096]{1,0:T(8,128)(2,1)} %q_hbm.1, bf16[32,256]{1,0:T(8,128)(2,1)} %sk_hbm.1, bf16[32,256]{1,0:T(8,128)(2,1)} %sv_hbm.1, bf16[2048,256]{1,0:T(8,128)(2,1)} %ck_hbm.1, bf16[2048,256]{1,0:T(8,128)(2,1)} %cv_hbm.1), custom_call_target="tpu_custom_call" | custom-call | tf_op jit(solution)/shard_map/pallas_call | solution.py:233
  16.3 0.7 %copy.10 = bf16[32,4096]{1,0:T(8,128)(2,1)} copy(bf16[32,4096]{1,0:T(8,128)(2,1)S(1)} %shard_map.82) | data formatting | bytes 524288
